TPU v7x, 512 devices: a whole 4x4x16 slice. The times are simulated.
512 devices in a mesh: past: 8 (over y, core), second: 64 (over z, x).
Axes of the slice: x: 4, y: 4, z: 16, core: 2. Of those that a mesh axis runs over, the one named last changes fastest.
Arguments:
- green_row: float32 [1024, 64, 128], P('second'), may hold values from -4 to 4
- green_hist: float32 [32, 1024, 64, 128], P('past', 'second'), may hold values from -5.25 to 5.25, as said below
- hamiltonian: float32 [64, 128], replicated, may hold values from -0.75 to 0.75
- quad_table: float32 [8], replicated, may hold values from 0.2 to 2
- weight_index: int32 [32], P('past'), may hold values from 0 to 7
- block_start: int32 [1], replicated, may hold values from 0 to 992
Outputs:
- green_next: float32 [1024, 64, 128], P('second')
- change_norm: float32 [1], replicated
Inputs may be any that keep to these rules, and one draw needn't show every extreme that they name: `green_hist`: real numbers of order one; magnitudes differ between second times.
All inputs are finite; a program needn't handle non-finite values.
Results may differ from a plain program's by a relative error of at most 0.0003.
Values sent between devices are 32-bit elements; how exact they have to be, the bound alone decides.
A program may use at most 64 MiB of HBM per device.

v0:
```python
import math
import jax
import jax.numpy as jnp
from jax import lax
from jax.sharding import PartitionSpec as P

coupling = 0.5
step_size = 0.25


def rotate(tiles, orbits):
    return jnp.concatenate([-tiles[..., orbits:], tiles[..., :orbits]], axis=-1)


def self_energy(tiles, orbits):
    magnitude = tiles[..., :orbits] ** 2 + tiles[..., orbits:] ** 2
    return -coupling * jnp.concatenate([magnitude, magnitude], axis=-1) * tiles


def local(green_row, green_hist, hamiltonian, quad_table, weight_index, block_start):
    orbits = hamiltonian.shape[0]
    sec_rows = green_row.shape[0]
    past_rows = green_hist.shape[0]
    total_past = past_rows * lax.axis_size("past")
    window_start = block_start[0]
    offset = lax.axis_index("second") * sec_rows
    past_first = lax.axis_index("past") * past_rows
    weights = jnp.take(quad_table, weight_index, axis=0)
    norm_scale = 1.0 / math.sqrt(orbits * total_past)
    ham_real = hamiltonian[:, :orbits]
    ham_imag = hamiltonian[:, orbits:]
    herm_real = 0.5 * (ham_real + ham_real.T)
    herm_imag = 0.5 * (ham_imag - ham_imag.T)
    right_side = jnp.stack([green_hist, self_energy(green_hist, orbits)])

    def select(tiles_in, wanted):
        local_pos = wanted - offset
        inside = (local_pos >= 0) & (local_pos < sec_rows)
        picked = jnp.take(tiles_in, jnp.clip(local_pos, 0, sec_rows - 1), axis=0)
        return jnp.where(inside[:, None, None], picked, jnp.zeros_like(picked))

    def window_of(tiles_in):
        wanted = window_start + jnp.arange(total_past, dtype=jnp.int32)
        every_tile = lax.psum(select(tiles_in, wanted), "second")
        return lax.dynamic_slice_in_dim(every_tile, past_first, past_rows, 0)

    def memory(tiles_in):
        window = window_of(tiles_in)
        weight_col = weights[:, None, None]
        left_side = jnp.stack([weight_col * self_energy(window, orbits), weight_col * window])
        left_side = jnp.stack([left_side[..., :orbits], left_side[..., orbits:]])
        contracted = jnp.einsum(
            "cqpij,qpsjk->csik", left_side, right_side, precision=lax.Precision.HIGHEST
        )
        return norm_scale * (contracted[0] + rotate(contracted[1], orbits))

    def derive(tiles_in, integral):
        first = jnp.einsum("ij,sjk->sik", herm_real, tiles_in, precision=lax.Precision.HIGHEST)
        second = jnp.einsum(
            "ij,sjk->sik", herm_imag, rotate(tiles_in, orbits), precision=lax.Precision.HIGHEST
        )
        combined = first + second + integral
        return jnp.concatenate([combined[..., orbits:], -combined[..., :orbits]], axis=-1)

    def summed(tiles_in):
        return lax.psum(memory(tiles_in), "past")

    slope_one = derive(green_row, summed(green_row))
    predicted = green_row + step_size * slope_one
    slope_two = derive(predicted, summed(predicted))
    green_next = green_row + 0.5 * step_size * (slope_one + slope_two)
    square_sum = lax.psum(jnp.sum((green_next - predicted) ** 2), "second")
    entry_count = sec_rows * lax.axis_size("second") * orbits * 2 * orbits
    change = jnp.sqrt(square_sum / entry_count) / step_size
    return (green_next, change.reshape(1))


def solution(mesh):
    placed = (P("second", None, None), P("past", "second", None, None), P(), P(), P("past"), P())
    return jax.shard_map(
        local, mesh=mesh, in_specs=placed, out_specs=(P("second", None, None), P()), check_vma=False
    )
```

profile of v0, /device:TPU:8, one launch (start us, length us, event | category | flops | bytes accessed | tf_op | source)
XLA Modules:
  0.0 879.2 jit_solution(6266481443964720765)
XLA Ops:
  7.9 1.7 gather_fusion.1
  9.6 1.2 select_select_fusion.1
  11.6 1.0 slice_negate_fusion.5
  13.1 2.7 copy_bitcast_fusion
  15.8 273.4 %all-reduce.5.cloned.1.call-done = f32[32,64,128]{2,1,0:T(8,128)} async-done(((f32[32,64,128]{2,1,0:T(8,128)}), f32[32,64,128]{2,1,0:T(8,128)}) %all-reduce.5.cloned.1.call-update) | async-done | bytes 1048592 | tf_op jit(solution)/shard_map/psum | solution.py:44
  289.2 1.1 fusion.28
  290.3 1.0 fusion.31
  291.5 4.4 fusion.5
  296.2 1.0 fusion.14
  297.5 0.7 convolution_bitcast_fusion
  298.3 67.6 %all-reduce.7.cloned.1.call-done = f32[16,64,128]{2,1,0:T(8,128)} async-done(((f32[16,64,128]{2,1,0:T(8,128)}), f32[16,64,128]{2,1,0:T(8,128)}) %all-reduce.7.cloned.1.call-update) | async-done | bytes 524304 | tf_op jit(solution)/shard_map/psum | solution.py:66
  365.9 1.6 fusion.8
  367.8 0.8 copy-done.4
  369.6 1.2 select_select_fusion
  370.9 1.4 fusion.38
  372.3 273.5 %all-reduce.9.cloned.1.call-done = f32[32,64,128]{2,1,0:T(8,128)} async-done(((f32[32,64,128]{2,1,0:T(8,128)}), f32[32,64,128]{2,1,0:T(8,128)}) %all-reduce.9.cloned.1.call-update) | async-done | bytes 1048592 | tf_op jit(solution)/shard_map/psum | solution.py:44
  645.8 1.1 fusion.27
  646.8 1.0 fusion.34
  648.0 4.1 fusion.6
  652.4 1.0 fusion.12
  653.7 68.5 %all-reduce.11.cloned.1.call-done = f32[16,64,128]{2,1,0:T(8,128)} async-done(((f32[16,64,128]{2,1,0:T(8,128)}), f32[16,64,128]{2,1,0:T(8,128)}) %all-reduce.11.cloned.1.call-update) | async-done | bytes 524304 | tf_op jit(solution)/shard_map/psum | solution.py:66
  722.2 1.9 fusion.10
  724.3 1.8 multiply_reduce_fusion
  726.1 144.7 %psum.39 = f32[]{:T(128)} all-reduce(f32[]{:T(128)} %get-tuple-element.3), channel_id=1, replica_groups=mesh['past'=8,'second'=64] {'second'}, use_global_device_ids=true, to_apply=%region_5.7 | all-reduce | flops 1 | bytes 8 | tf_op jit(solution)/shard_map/psum | solution.py:72
  (52 shorter events, 4.2 us)
Async XLA Ops:
  7.2 3.7 copy-start
  7.2 282.0 %all-reduce.5.cloned.1.call-start = ((), (), s32[]{:S(2)}) async-start(), calls=%async_computation | async-start | bytes 2097152 | tf_op jit(solution)/shard_map/psum | solution.py:44
  9.6 1.3 copy-start.11
  9.6 2.0 copy-start.1
  10.8 1.7 copy-start.2
  10.8 355.1 %all-reduce.7.cloned.1.call-start = ((), (), s32[]{:S(2)}) async-start(), calls=%async_computation.1 | async-start | bytes 1048576 | tf_op jit(solution)/shard_map/psum | solution.py:66
  296.0 1.3 copy-start.10
  296.0 1.6 copy-start.8
  297.2 348.5 %all-reduce.9.cloned.1.call-start = ((), (), s32[]{:S(2)}) async-start(), calls=%async_computation.2 | async-start | bytes 2097152 | tf_op jit(solution)/shard_map/psum | solution.py:44
  367.8 0.8 copy-start.4
  367.8 1.0 copy-start.6
  370.8 277.2 %copy-start.3 = (f32[1,4,16,64,128]{4,3,0,1,2:T(8,128)S(1)}, f32[1,4,16,64,128]{4,3,0,1,2:T(8,128)}, u32[]{:S(2)}) copy-start(f32[1,4,16,64,128]{4,3,0,1,2:T(8,128)} %get-tuple-element.7) | copy-start | bytes 6291460
  370.8 351.4 %all-reduce.11.cloned.1.call-start = ((), (), s32[]{:S(2)}) async-start(), calls=%async_computation.3 | async-start | bytes 1048576 | tf_op jit(solution)/shard_map/psum | solution.py:66
  652.4 69.8 %copy-start.9 = (f32[16,128,64]{1,2,0:T(8,128)S(1)}, f32[16,128,64]{1,2,0:T(8,128)}, u32[]{:S(2)}) copy-start(f32[16,128,64]{1,2,0:T(8,128)} %fusion.38) | copy-start | bytes 1572868
  722.2 2.1 copy-start.5
  722.2 2.1 copy-start.7
Sparse Core Ops, SparseCore 0:
  11.4 277.7 all-reduce.4
  297.4 68.5 all-reduce.6
  370.9 274.7 all-reduce.8
  653.6 68.5 all-reduce.10
where the time goes:
time: 880 us; the launch traced here: 879 us
  waiting for transfers between devices  683 us (78%)
  blocking collectives  145 us (16%)
  between operations  16.5 us (2%)
  other arithmetic  16.1 us (2%)
  matrix products  14.3 us (2%)
    psum x2, waiting for transfers between devices, window_of(): every_tile = lax.psum(select(tiles_in, wanted), 'second')  547 us
    psum x1, blocking collectives, local(): square_sum = lax.psum(jnp.sum((green_next - predicted) ** 2), 'second')  145 us
    psum x2, waiting for transfers between devices, summed(): return lax.psum(memory(tiles_in), 'past')  136 us
  transfers between devices with their start and end apart: 4, of which 4 were waited for; matrix products, arithmetic and copies ran while one was open for 1% of the time, Pallas kernels for 0%

commit v1 on v0

--- a/solution.py
+++ b/solution.py
@@ -1,3 +1,4 @@
+import functools
 import math
 import jax
 import jax.numpy as jnp
@@ -6,6 +7,14 @@
 
 coupling = 0.5
 step_size = 0.25
+
+
+def convert_points(local_values, across):
+    view_out = jnp.sum(lax.all_gather(local_values, axis_name=across), 0)
+    return view_out
+
+
+unit_store = functools.partial(convert_points, across="past")
 
 
 def rotate(tiles, orbits):
@@ -63,7 +72,7 @@
         return jnp.concatenate([combined[..., orbits:], -combined[..., :orbits]], axis=-1)
 
     def summed(tiles_in):
-        return lax.psum(memory(tiles_in), "past")
+        return unit_store(memory(tiles_in))
 
     slope_one = derive(green_row, summed(green_row))
     predicted = green_row + step_size * slope_one

time: 880 us -> 816 us (0.927)
  waiting for transfers between devices: 683 us -> 613 us
    psum x2 -> x0, waiting for transfers between devices: 136 us -> none  [summed(): return lax.psum(memory(tiles_in), 'past')]
    all_gather x0 -> x2, waiting for transfers between devices: none -> 64.8 us  [convert_points(): view_out = jnp.sum(lax.all_gather(local_values, axis_name=across), 0)]
where the time goes in v1:
time: 816 us
  waiting for transfers between devices  613 us (75%)
  blocking collectives  145 us (18%)
  other arithmetic  23.4 us (3%)
  between operations  16.5 us (2%)
  matrix products  11.2 us (1%)
    psum x2, waiting for transfers between devices, window_of(): every_tile = lax.psum(select(tiles_in, wanted), 'second')  548 us
    psum x1, blocking collectives, local(): square_sum = lax.psum(jnp.sum((green_next - predicted) ** 2), 'second')  145 us
    all_gather x2, waiting for transfers between devices, convert_points(): view_out = jnp.sum(lax.all_gather(local_values, axis_name=across), 0)  64.8 us
  transfers between devices with their start and end apart: 4, of which 4 were waited for; matrix products, arithmetic and copies ran while one was open for 1% of the time, Pallas kernels for 0%

profile of v1, /device:TPU:8, one launch (start us, length us, event | category | flops | bytes accessed | tf_op | source)
XLA Modules:
  0.0 815.7 jit_solution(17675886641032141502)
XLA Ops:
  7.9 2.6 gather_fusion.1
  10.5 2.5 select_select_fusion.1
  14.5 2.7 copy_bitcast_fusion
  17.1 273.9 %all-reduce.3.cloned.1.call-done = f32[32,64,128]{2,1,0:T(8,128)} async-done(((f32[32,64,128]{2,1,0:T(8,128)}), f32[32,64,128]{2,1,0:T(8,128)}) %all-reduce.3.cloned.1.call-update) | async-done | bytes 1048592 | tf_op jit(solution)/shard_map/psum | solution.py:53
  291.0 1.1 fusion.36
  292.1 1.0 fusion.39
  293.2 4.4 fusion.10
  298.0 1.0 fusion.21
  299.5 0.7 convolution_bitcast_fusion
  300.3 32.2 %all-gather.3.cloned.1.call-done = f32[8,16,64,128]{3,2,1,0:T(8,128)} async-done(((f32[1,16,64,128]{3,2,1,0:T(8,128)}), f32[8,16,64,128]{3,2,1,0:T(8,128)}) %all-gather.3.cloned.1.call-update) | async-done | bytes 4194320 | tf_op jit(solution)/shard_map/all_gather | solution.py:13
  332.5 2.6 reduce_sum.27
  335.9 0.8 copy-done.4
  337.1 1.6 gather_fusion.2
  338.7 2.6 select_select_fusion
  341.5 274.3 %all-reduce.5.cloned.1.call-done = f32[32,64,128]{2,1,0:T(8,128)} async-done(((f32[32,64,128]{2,1,0:T(8,128)}), f32[32,64,128]{2,1,0:T(8,128)}) %all-reduce.5.cloned.1.call-update) | async-done | bytes 1048592 | tf_op jit(solution)/shard_map/psum | solution.py:53
  615.8 1.1 fusion.35
  616.9 1.0 fusion.42
  618.1 4.1 fusion.7
  622.5 1.0 fusion.18
  624.4 32.6 %all-gather.5.cloned.1.call-done = f32[8,16,64,128]{3,2,1,0:T(8,128)} async-done(((f32[1,16,64,128]{3,2,1,0:T(8,128)}), f32[8,16,64,128]{3,2,1,0:T(8,128)}) %all-gather.5.cloned.1.call-update) | async-done | bytes 4194320 | tf_op jit(solution)/shard_map/all_gather | solution.py:13
  657.0 2.6 reduce_sum.28
  659.6 0.8 fusion.16
  660.8 1.8 multiply_reduce_fusion
  662.6 144.7 %psum.23 = f32[]{:T(128)} all-reduce(f32[]{:T(128)} %get-tuple-element.3), channel_id=1, replica_groups=mesh['past'=8,'second'=64] {'second'}, use_global_device_ids=true, to_apply=%region_5.7 | all-reduce | flops 1 | bytes 8 | tf_op jit(solution)/shard_map/psum | solution.py:81
  (50 shorter events, 5.3 us)
Async XLA Ops:
  7.2 6.0 copy-start
  7.2 283.8 %all-reduce.3.cloned.1.call-start = ((), (), s32[]{:S(2)}) async-start(), calls=%async_computation | async-start | bytes 2097152 | tf_op jit(solution)/shard_map/psum | solution.py:53
  10.5 2.6 copy-start.9
  10.5 3.3 copy-start.2
  13.1 319.4 %all-gather.3.cloned.1.call-start = ((), (), s32[]{:S(2)}) async-start(), calls=%async_computation.1 | async-start | bytes 4718592 | tf_op jit(solution)/shard_map/all_gather | solution.py:13
  297.7 1.3 copy-start.8
  297.7 1.6 copy-start.1
  299.0 316.8 %all-reduce.5.cloned.1.call-start = ((), (), s32[]{:S(2)}) async-start(), calls=%async_computation.2 | async-start | bytes 2097152 | tf_op jit(solution)/shard_map/psum | solution.py:53
  335.9 0.8 copy-start.4
  335.9 1.0 copy-start.6
  338.7 279.4 %copy-start.3 = (f32[1,4,16,64,128]{4,3,0,1,2:T(8,128)S(1)}, f32[1,4,16,64,128]{4,3,0,1,2:T(8,128)}, u32[]{:S(2)}) copy-start(f32[1,4,16,64,128]{4,3,0,1,2:T(8,128)} %get-tuple-element.7) | copy-start | bytes 6291460
  341.3 315.7 %all-gather.5.cloned.1.call-start = ((), (), s32[]{:S(2)}) async-start(), calls=%async_computation.3 | async-start | bytes 4718592 | tf_op jit(solution)/shard_map/all_gather | solution.py:13
  659.6 1.0 copy-start.5
  659.6 1.2 copy-start.7
Sparse Core Ops, SparseCore 0:
  13.2 277.7 all-reduce.2
  299.1 33.3 all-gather.2
  341.4 274.3 all-reduce.4
  623.6 33.3 all-gather.4
